TPU v7x, 32 devices: a whole 2x2x4 slice. The times are simulated.
32 devices in a mesh: subtree: 2 (over x), panel: 4 (over y, core), snap: 4 (over z).
Axes of the slice: x: 2, y: 2, z: 4, core: 2. Of those that a mesh axis runs over, the one named last changes fastest.
Arguments:
- leaf_rhs: bfloat16 [8, 1024, 128], P('subtree', 'panel', 'snap'), may hold values from -6 to 6
- upper_rhs: bfloat16 [7, 1024, 128], P(None, 'panel', 'snap'), may hold values from -6 to 6
- leaf_inv: bfloat16 [8, 1024, 1024], P('subtree', 'panel'), may hold values from -1 to 2, as said below
- upper_inv: bfloat16 [7, 1024, 1024], P(None, 'panel'), may hold values from -1 to 2, as said below
- leaf_panels: bfloat16 [8, 3, 1024, 1024], P('subtree', None, 'panel'), may hold values from -0.09375 to 0.09375
- mid_panels: bfloat16 [4, 2, 1024, 1024], P(None, None, 'panel'), may hold values from -0.09375 to 0.09375
- top_panels: bfloat16 [2, 1024, 1024], P(None, 'panel'), may hold values from -0.09375 to 0.09375
- leaf_widths: int32 [8], P('subtree'), may hold values from 256 to 1024
- upper_widths: int32 [7], replicated, may hold values from 256 to 1024
Outputs:
- leaf_solution: bfloat16 [8, 1024, 128], P('subtree', 'panel', 'snap')
- upper_solution: bfloat16 [7, 1024, 128], P(None, 'panel', 'snap')
Inputs may be any that keep to these rules, and one draw needn't show every extreme that they name: `leaf_inv`: each inverse block is a full matrix near the identity. `upper_inv`: each inverse block is a full matrix near the identity.
All inputs are finite; a program needn't handle non-finite values.
Results may differ from a plain program's by a relative error of at most 0.024.
Values may be sent and summed in bfloat16 or wider, within the bound.
A program may use at most 64 MiB of HBM per device.

v0:
```python
import jax
import jax.numpy as jnp
from jax import lax
from jax.sharding import PartitionSpec as P


def live_mask(widths, full_width):
    return (jnp.arange(full_width, dtype=jnp.int32)[None, :] < widths[:, None]).astype(jnp.float32)


def own_rows(mask_full, own_count):
    return lax.dynamic_slice_in_dim(mask_full, lax.axis_index("panel") * own_count, own_count, 1)


def solve_down(inverse, reduced, mask_full):
    own_count = inverse.shape[1]
    live_cols = mask_full.astype(jnp.bfloat16)
    result = jnp.einsum(
        "nrw,nwc->nrc",
        inverse,
        lax.all_gather(reduced, "panel", axis=1, tiled=True) * live_cols[:, :, None],
        preferred_element_type=jnp.float32,
    )
    return (result * own_rows(mask_full, own_count)[:, :, None]).astype(jnp.bfloat16)


def spread(panels, solved):
    return jnp.einsum(
        "nkrw,nwc->nkrc",
        panels,
        lax.all_gather(solved, "panel", axis=1, tiled=True),
        preferred_element_type=jnp.float32,
    )


def ancestor_tables(global_index, level, count_up):
    offsets = [0, 0, 4, 6]
    slot_ids = jnp.arange(7, dtype=jnp.int32)
    tables = []
    for ancestor_rank in range(count_up):
        target = offsets[level + 1 + ancestor_rank] + jnp.right_shift(
            global_index, 1 + ancestor_rank
        )
        tables.append((slot_ids[None, :] == target[:, None]).astype(jnp.float32))
    return tables


def add_coupled(accum, coupled, tables):
    for ancestor_rank in range(len(tables)):
        accum = accum + jnp.einsum(
            "nrc,nu->urc",
            coupled[:, ancestor_rank],
            tables[ancestor_rank],
            precision=lax.Precision.HIGHEST,
        )
    return accum


def solve_up(inverse, panels, solved, upper_x, tables, mask_full):
    own_count = inverse.shape[1]
    if panels is None:
        reduced = solved
    else:
        picked = jnp.stack(
            [
                jnp.einsum(
                    "nu,urc->nrc",
                    table.astype(jnp.bfloat16),
                    upper_x,
                    preferred_element_type=jnp.float32,
                ).astype(jnp.bfloat16)
                for table in tables
            ],
            axis=1,
        )
        carried = lax.psum_scatter(
            jnp.einsum("nkrw,nkrc->wnc", panels, picked, preferred_element_type=jnp.float32).astype(
                jnp.bfloat16
            ),
            "panel",
            scatter_dimension=0,
            tiled=True,
        ).astype(jnp.float32)
        reduced = (solved.astype(jnp.float32) - jnp.transpose(carried, (1, 0, 2))).astype(
            jnp.bfloat16
        )
    own_live = own_rows(mask_full, own_count)
    masked = reduced * own_live[:, :, None].astype(jnp.bfloat16)
    summed = lax.psum_scatter(
        jnp.einsum("nrw,nrc->wnc", inverse, masked, preferred_element_type=jnp.float32).astype(
            jnp.bfloat16
        ),
        "panel",
        scatter_dimension=0,
        tiled=True,
    ).astype(jnp.float32)
    return (jnp.transpose(summed, (1, 0, 2)) * own_live[:, :, None]).astype(jnp.bfloat16)


def per_device(
    leaf_rhs,
    upper_rhs,
    leaf_inv,
    upper_inv,
    leaf_panels,
    mid_panels,
    top_panels,
    leaf_widths,
    upper_widths,
):
    full_width = leaf_inv.shape[2]
    own_count = leaf_inv.shape[1]
    leaf_count = leaf_inv.shape[0]
    groups = lax.axis_size("subtree")
    group_id = lax.axis_index("subtree")
    leaf_live = live_mask(leaf_widths, full_width)
    upper_live = live_mask(upper_widths, full_width)
    leaf_index = group_id * leaf_count + jnp.arange(leaf_count, dtype=jnp.int32)
    upper_index = jnp.arange(7, dtype=jnp.int32)
    leaf_tables = ancestor_tables(leaf_index, 0, 3)
    mid_tables = ancestor_tables(upper_index[0:4], 1, 2)
    high_tables = ancestor_tables(upper_index[4:6] - 4, 2, 1)
    top_stack = top_panels[:, None]
    leaf_sol = solve_down(leaf_inv, leaf_rhs, leaf_live)
    coupled_sum = jnp.zeros((7, own_count, leaf_rhs.shape[2]), jnp.float32)
    coupled_sum = add_coupled(coupled_sum, spread(leaf_panels, leaf_sol), leaf_tables)
    column_share = leaf_rhs.shape[2] // groups
    coupled_sum = lax.psum_scatter(
        coupled_sum.astype(jnp.bfloat16), "subtree", scatter_dimension=2, tiled=True
    ).astype(jnp.float32)
    upper_part = lax.dynamic_slice_in_dim(upper_rhs, group_id * column_share, column_share, 2)
    mid_sol = solve_down(
        upper_inv[0:4],
        (upper_part[0:4].astype(jnp.float32) - coupled_sum[0:4]).astype(jnp.bfloat16),
        upper_live[0:4],
    )
    coupled_sum = add_coupled(coupled_sum, spread(mid_panels, mid_sol), mid_tables)
    high_sol = solve_down(
        upper_inv[4:6],
        (upper_part[4:6].astype(jnp.float32) - coupled_sum[4:6]).astype(jnp.bfloat16),
        upper_live[4:6],
    )
    coupled_sum = add_coupled(coupled_sum, spread(top_stack, high_sol), high_tables)
    root_sol = solve_down(
        upper_inv[6:7],
        (upper_part[6:7].astype(jnp.float32) - coupled_sum[6:7]).astype(jnp.bfloat16),
        upper_live[6:7],
    )
    column_count = upper_part.shape[2]
    zero_mid = jnp.zeros((4, own_count, column_count), jnp.bfloat16)
    zero_high = jnp.zeros((2, own_count, column_count), jnp.bfloat16)
    root_x = solve_up(upper_inv[6:7], None, root_sol, None, None, upper_live[6:7])
    upper_x = jnp.concatenate([zero_mid, zero_high, root_x], axis=0)
    high_x = solve_up(upper_inv[4:6], top_stack, high_sol, upper_x, high_tables, upper_live[4:6])
    upper_x = jnp.concatenate([zero_mid, high_x, root_x], axis=0)
    mid_x = solve_up(upper_inv[0:4], mid_panels, mid_sol, upper_x, mid_tables, upper_live[0:4])
    upper_x = jnp.concatenate([mid_x, high_x, root_x], axis=0)
    upper_x = lax.all_gather(upper_x, "subtree", axis=2, tiled=True)
    leaf_x = solve_up(leaf_inv, leaf_panels, leaf_sol, upper_x, leaf_tables, leaf_live)
    return (leaf_x, upper_x)


def solution(mesh):
    in_specs = (
        P("subtree", "panel", "snap"),
        P(None, "panel", "snap"),
        P("subtree", "panel", None),
        P(None, "panel", None),
        P("subtree", None, "panel", None),
        P(None, None, "panel", None),
        P(None, "panel", None),
        P("subtree"),
        P(),
    )
    out_specs = (P("subtree", "panel", "snap"), P(None, "panel", "snap"))
    return jax.shard_map(
        per_device, mesh=mesh, in_specs=in_specs, out_specs=out_specs, check_vma=False
    )
```

profile of v0, /device:TPU:0, one launch (start us, length us, event | category | flops | bytes accessed | tf_op | source)
XLA Modules:
  0.0 253.7 jit_solution(11947335732800104918)
XLA Ops:
  7.3 0.9 fusion.93
  8.1 7.4 %all_gather.24 = bf16[4,1024,32]{1,2,0:T(8,128)(2,1)S(1)} all-gather(bf16[4,256,32]{1,2,0:T(8,128)(2,1)} %param.9), channel_id=1, replica_groups=mesh['subtree'=2,'panel'=4,'snap'=4] {'panel'}, dimensions={1}, use_global_device_ids=true | all-gather | bytes 327680 | tf_op jit(solution)/shard_map/all_gather | solution.py:21
  15.6 0.7 fusion.22
  16.3 5.9 %all_gather.25 = bf16[4,1024,32]{1,2,0:T(8,128)(2,1)S(1)} all-gather(bf16[4,256,32]{1,2,0:T(8,128)(2,1)S(1)} %fusion.22), channel_id=1, replica_groups=mesh['subtree'=2,'panel'=4,'snap'=4] {'panel'}, dimensions={1}, use_global_device_ids=true | all-gather | bytes 327680 | tf_op jit(solution)/shard_map/all_gather | solution.py:31
  22.1 4.8 %convolution_bitcast_fusion.1 = f32[4,3,256,32]{2,3,1,0:T(8,128)S(1)} fusion(bf16[4,3,256,1024]{3,2,1,0:T(8,128)(2,1)} %param.13, bf16[4,1024,32]{1,2,0:T(8,128)(2,1)S(1)} %all_gather.25), kind=kOutput, calls=%fused_computation.7 | convolution fusion | flops 201326592 | bytes 6946816 | tf_op jit(solution)/shard_map/nkrw,nwc->nkrc/dot_general | solution.py:28
  27.0 0.4 fusion.54
  27.4 0.4 convolution_add_fusion.1
  27.8 1.1 fusion.7
  29.3 11.3 %reduce-scatter.9.cloned.1.call-done = bf16[7,256,16]{1,0,2:T(8,128)(2,1)} async-done(((bf16[7,256,32]{1,0,2:T(8,128)(2,1)}), bf16[7,256,16]{1,0,2:T(8,128)(2,1)}) %reduce-scatter.9.cloned.1.call-update) | async-done | bytes 57360 | tf_op jit(solution)/shard_map/reduce_scatter | solution.py:128
  40.6 0.8 convert_element_type.246
  41.5 5.4 %all_gather.26 = bf16[4,1024,16]{1,0,2:T(4,128)(2,1)S(1)} all-gather(bf16[4,256,16]{1,0,2:T(4,128)(2,1)S(1)} %fusion.64), channel_id=1, replica_groups=mesh['subtree'=2,'panel'=4,'snap'=4] {'panel'}, dimensions={1}, use_global_device_ids=true | all-gather | bytes 163840 | tf_op jit(solution)/shard_map/all_gather | solution.py:21
  46.9 2.3 fusion.32
  49.2 5.6 %all_gather.27 = bf16[4,1024,16]{1,2,0:T(8,128)(2,1)S(1)} all-gather(bf16[4,256,16]{1,2,0:T(8,128)(2,1)S(1)} %fusion.32), channel_id=1, replica_groups=mesh['subtree'=2,'panel'=4,'snap'=4] {'panel'}, dimensions={1}, use_global_device_ids=true | all-gather | bytes 163840 | tf_op jit(solution)/shard_map/all_gather | solution.py:31
  54.8 3.4 %convolution_bitcast_fusion.3 = f32[4,2,256,16]{2,3,1,0:T(8,128)S(1)} fusion(bf16[4,2,256,1024]{3,2,1,0:T(8,128)(2,1)} %param.14, bf16[4,1024,16]{1,2,0:T(8,128)(2,1)S(1)} %all_gather.27), kind=kOutput, calls=%fused_computation.18 | convolution fusion | flops 67108864 | bytes 4456448 | tf_op jit(solution)/shard_map/nkrw,nwc->nkrc/dot_general | solution.py:28
  58.2 0.3 convolution_add_fusion.3
  58.5 0.3 convolution_add_fusion.2
  58.9 5.3 %all_gather.28 = bf16[2,1024,16]{1,0,2:T(2,128)(2,1)S(1)} all-gather(bf16[2,256,16]{1,0,2:T(2,128)(2,1)S(1)} %fusion.73), channel_id=1, replica_groups=mesh['subtree'=2,'panel'=4,'snap'=4] {'panel'}, dimensions={1}, use_global_device_ids=true | all-gather | bytes 81920 | tf_op jit(solution)/shard_map/all_gather | solution.py:21
  64.2 1.6 fusion.36
  65.8 5.2 %all_gather.29 = bf16[2,1024,16]{1,2,0:T(8,128)(2,1)S(1)} all-gather(bf16[2,256,16]{1,2,0:T(8,128)(2,1)S(1)} %fusion.36), channel_id=1, replica_groups=mesh['subtree'=2,'panel'=4,'snap'=4] {'panel'}, dimensions={1}, use_global_device_ids=true | all-gather | bytes 81920 | tf_op jit(solution)/shard_map/all_gather | solution.py:31
  71.0 0.4 fusion.142
  71.4 0.3 fusion.83
  71.8 5.3 %all_gather.30 = bf16[1,1024,16]{1,0,2:T(2,128)(2,1)S(1)} all-gather(bf16[1,256,16]{1,0,2:T(2,128)(2,1)S(1)} %fusion.94), channel_id=1, replica_groups=mesh['subtree'=2,'panel'=4,'snap'=4] {'panel'}, dimensions={1}, use_global_device_ids=true | all-gather | bytes 40960 | tf_op jit(solution)/shard_map/all_gather | solution.py:21
  77.1 2.4 fusion.31
  79.6 19.4 %reduce-scatter.11.cloned.1.call-done = bf16[256,1,16]{0,2,1:T(8,128)(2,1)} async-done(((bf16[1024,1,16]{0,2,1:T(8,128)(2,1)}), bf16[256,1,16]{0,2,1:T(8,128)(2,1)}) %reduce-scatter.11.cloned.1.call-update) | async-done | bytes 8208 | tf_op jit(solution)/shard_map/reduce_scatter | solution.py:89
  99.0 0.7 fusion.91
  99.7 0.2 fusion.61
  100.1 0.9 fusion.21
  101.1 20.6 %reduce-scatter.13.cloned.1.call-done = bf16[256,2,16]{0,2,1:T(8,128)(2,1)} async-done(((bf16[1024,2,16]{0,2,1:T(8,128)(2,1)}), bf16[256,2,16]{0,2,1:T(8,128)(2,1)}) %reduce-scatter.13.cloned.1.call-update) | async-done | bytes 16400 | tf_op jit(solution)/shard_map/reduce_scatter | solution.py:76
  121.6 2.1 fusion.17
  123.8 20.1 %reduce-scatter.15.cloned.1.call-done = bf16[256,2,16]{0,2,1:T(8,128)(2,1)} async-done(((bf16[1024,2,16]{0,2,1:T(8,128)(2,1)}), bf16[256,2,16]{0,2,1:T(8,128)(2,1)}) %reduce-scatter.15.cloned.1.call-update) | async-done | bytes 16400 | tf_op jit(solution)/shard_map/reduce_scatter | solution.py:89
  143.9 0.7 fusion.81
  144.7 0.2 fusion.29
  144.9 0.2 fusion.30
  145.2 3.5 %fusion.15 = bf16[1024,4,16]{0,2,1:T(8,128)(2,1)} fusion(bf16[4,2,256,1024]{3,2,1,0:T(8,128)(2,1)} %param.14, bf16[4,2,256,16]{2,0,3,1:T(4,128)(2,1)S(1)} %pad_maximum_fusion.4), kind=kOutput, calls=%fused_computation.21 | convolution fusion | flops 67174400 | bytes 4390912 | tf_op jit(solution)/shard_map/nkrw,nkrc->wnc/dot_general | solution.py:77
  148.7 19.7 %reduce-scatter.17.cloned.1.call-done = bf16[256,4,16]{0,2,1:T(8,128)(2,1)} async-done(((bf16[1024,4,16]{0,2,1:T(8,128)(2,1)}), bf16[256,4,16]{0,2,1:T(8,128)(2,1)}) %reduce-scatter.17.cloned.1.call-update) | async-done | bytes 32784 | tf_op jit(solution)/shard_map/reduce_scatter | solution.py:76
  168.4 2.6 %fusion.12 = bf16[1024,4,16]{0,2,1:T(8,128)(2,1)} fusion(bf16[7,256,1024]{2,1,0:T(8,128)(2,1)} %param.12, bf16[256,4,16]{0,2,1:T(8,128)(2,1)} %reduce-scatter.17.cloned.1.call-done, bf16[4,256,16]{1,2,0:T(8,128)(2,1)S(1)} %fusion.32, bf16[4,256]{1,0:T(4,128)(2,1)S(1)} %get-tuple-element.4), kind=kOutput, calls=%fused_computation.20 | convolution fusion | flops 33701888 | bytes 2295808 | tf_op jit(solution)/shard_map/nrw,nrc->wnc/dot_general | solution.py:90
  171.1 19.7 %reduce-scatter.19.cloned.1.call-done = bf16[256,4,16]{0,2,1:T(8,128)(2,1)} async-done(((bf16[1024,4,16]{0,2,1:T(8,128)(2,1)}), bf16[256,4,16]{0,2,1:T(8,128)(2,1)}) %reduce-scatter.19.cloned.1.call-update) | async-done | bytes 32784 | tf_op jit(solution)/shard_map/reduce_scatter | solution.py:89
  190.8 0.8 fusion.65
  191.6 4.9 %all_gather.31 = bf16[7,256,32]{1,2,0:T(8,128)(2,1)S(1)} all-gather(bf16[7,256,16]{1,2,0:T(8,128)(2,1)S(1)} %pad_maximum_fusion.5), channel_id=1, replica_groups=mesh['subtree'=2,'panel'=4,'snap'=4] {'subtree'}, dimensions={2}, use_global_device_ids=true | all-gather | bytes 172032 | tf_op jit(solution)/shard_map/all_gather | solution.py:158
  196.4 0.2 fusion.18
  196.7 0.2 fusion.19
  196.9 0.2 fusion.20
  197.3 4.7 %fusion.5 = bf16[1024,4,32]{0,2,1:T(8,128)(2,1)} fusion(bf16[4,3,256,1024]{3,2,1,0:T(8,128)(2,1)} %param.13, bf16[4,3,256,32]{2,0,3,1:T(4,128)(2,1)S(1)} %pad_maximum_fusion), kind=kOutput, calls=%fused_computation.8 | convolution fusion | flops 201457664 | bytes 6750208 | tf_op jit(solution)/shard_map/nkrw,nkrc->wnc/dot_general | solution.py:77
  202.1 20.1 %reduce-scatter.21.cloned.1.call-done = bf16[256,4,32]{0,2,1:T(8,128)(2,1)} async-done(((bf16[1024,4,32]{0,2,1:T(8,128)(2,1)}), bf16[256,4,32]{0,2,1:T(8,128)(2,1)}) %reduce-scatter.21.cloned.1.call-update) | async-done | bytes 65552 | tf_op jit(solution)/shard_map/reduce_scatter | solution.py:76
  222.2 2.0 fusion.6
  224.2 20.5 %reduce-scatter.23.cloned.1.call-done = bf16[256,4,32]{0,2,1:T(8,128)(2,1)} async-done(((bf16[1024,4,32]{0,2,1:T(8,128)(2,1)}), bf16[256,4,32]{0,2,1:T(8,128)(2,1)}) %reduce-scatter.23.cloned.1.call-update) | async-done | bytes 65552 | tf_op jit(solution)/shard_map/reduce_scatter | solution.py:89
  244.8 1.5 fusion.49
  246.2 0.6 copy.93
  (66 shorter events, 1.5 us)
Async XLA Ops:
  7.2 8.4 %copy-start = (bf16[4,256,1024]{2,1,0:T(8,128)(2,1)S(1)}, bf16[4,256,1024]{2,1,0:T(8,128)(2,1)}, u32[]{:S(2)}) copy-start(bf16[4,256,1024]{2,1,0:T(8,128)(2,1)} %param.11) | copy-start | bytes 6291460
  7.2 33.4 %reduce-scatter.9.cloned.1.call-start = ((), (), s32[]{:S(2)}) async-start(), calls=%async_computation.8 | async-start | bytes 196608 | tf_op jit(solution)/shard_map/reduce_scatter | solution.py:128
  22.1 6.8 %copy-start.4 = (s32[7]{0:T(128)S(1)}, s32[7]{0:T(128)}, u32[]{:S(2)}) copy-start(s32[7]{0:T(128)} %param.17) | copy-start | bytes 88
  22.1 6.9 %copy-start.3 = (bf16[7,256,32]{1,2,0:T(8,128)(2,1)S(1)}, bf16[7,256,32]{1,2,0:T(8,128)(2,1)}, u32[]{:S(2)}) copy-start(bf16[7,256,32]{1,2,0:T(8,128)(2,1)} %param.10) | copy-start | bytes 344068
  28.9 70.1 %reduce-scatter.11.cloned.1.call-start = ((), (), s32[]{:S(2)}) async-start(), calls=%async_computation.9 | async-start | bytes 40960 | tf_op jit(solution)/shard_map/reduce_scatter | solution.py:89
  46.9 11.3 %copy-start.2 = (bf16[7,256,16]{1,0,2:T(8,128)(2,1)S(1)}, bf16[7,256,16]{1,0,2:T(8,128)(2,1)}, u32[]{:S(2)}) copy-start(bf16[7,256,16]{1,0,2:T(8,128)(2,1)} %reduce-scatter.9.cloned.1.call-done) | copy-start | bytes 172036
  49.2 21.8 %copy-start.1 = (bf16[2,256,1024]{2,1,0:T(8,128)(2,1)S(1)}, bf16[2,256,1024]{2,1,0:T(8,128)(2,1)}, u32[]{:S(2)}) copy-start(bf16[2,256,1024]{2,1,0:T(8,128)(2,1)} %param.15) | copy-start | bytes 3145732
  79.5 42.1 %reduce-scatter.13.cloned.1.call-start = ((), (), s32[]{:S(2)}) async-start(), calls=%async_computation.10 | async-start | bytes 81920 | tf_op jit(solution)/shard_map/reduce_scatter | solution.py:76
  101.0 42.9 %reduce-scatter.15.cloned.1.call-start = ((), (), s32[]{:S(2)}) async-start(), calls=%async_computation.11 | async-start | bytes 81920 | tf_op jit(solution)/shard_map/reduce_scatter | solution.py:89
  123.8 44.6 %reduce-scatter.17.cloned.1.call-start = ((), (), s32[]{:S(2)}) async-start(), calls=%async_computation.12 | async-start | bytes 163840 | tf_op jit(solution)/shard_map/reduce_scatter | solution.py:76
  148.7 42.1 %reduce-scatter.19.cloned.1.call-start = ((), (), s32[]{:S(2)}) async-start(), calls=%async_computation.13 | async-start | bytes 163840 | tf_op jit(solution)/shard_map/reduce_scatter | solution.py:89
  171.1 51.1 %reduce-scatter.21.cloned.1.call-start = ((), (), s32[]{:S(2)}) async-start(), calls=%async_computation.14 | async-start | bytes 327680 | tf_op jit(solution)/shard_map/reduce_scatter | solution.py:76
  202.0 42.7 %reduce-scatter.23.cloned.1.call-start = ((), (), s32[]{:S(2)}) async-start(), calls=%async_computation.15 | async-start | bytes 327680 | tf_op jit(solution)/shard_map/reduce_scatter | solution.py:89
Sparse Core Ops, SparseCore 0:
  29.0 11.5 reduce-scatter.8
  79.6 19.3 reduce-scatter.10
  102.1 19.4 reduce-scatter.12
  124.5 19.4 reduce-scatter.14
  148.8 19.5 reduce-scatter.16
  171.2 19.5 reduce-scatter.18
  202.1 20.0 reduce-scatter.20
  224.7 20.0 reduce-scatter.22
where the time goes:
time: 255 us; the launch traced here: 254 us
  waiting for transfers between devices  151 us (59%)
  blocking collectives  44.9 us (18%)
  matrix products  35.5 us (14%)
  between operations  14.5 us (6%)
  other arithmetic  6.07 us (2%)
    reduce_scatter x4, waiting for transfers between devices, solve_up(): lax.psum_scatter(jnp.einsum('nrw,nrc->wnc', inverse, masked, preferred_el...  79.6 us
    reduce_scatter x3, waiting for transfers between devices, solve_up(): lax.psum_scatter(jnp.einsum('nkrw,nkrc->wnc', panels, picked, preferred_e...  60.4 us
    all_gather x4, blocking collectives, solve_down(): lax.all_gather(reduced, 'panel', axis=1, tiled=True) * live_cols[:, :, None]  23.4 us
    all_gather x3, blocking collectives, spread(): lax.all_gather(solved, 'panel', axis=1, tiled=True)  16.7 us
    reduce_scatter x1, waiting for transfers between devices, per_device(): lax.psum_scatter(coupled_sum.astype(jnp.bfloat16), 'subtree', scatter_dim...  11.3 us
    dot_general x4, matrix products, solve_up(): jnp.einsum('nrw,nrc->wnc', inverse, masked, preferred_element_type=jnp.fl...  9.13 us
    dot_general x3, matrix products, solve_up(): jnp.einsum('nkrw,nkrc->wnc', panels, picked, preferred_element_type=jnp.f...  9.09 us
    dot_general x3, matrix products, spread(): jnp.einsum('nkrw,nwc->nkrc', panels, lax.all_gather(solved, 'panel', axis...  8.51 us
  transfers between devices with their start and end apart: 8, of which 8 were waited for; matrix products, arithmetic and copies ran while one was open for 0% of the time, Pallas kernels for 0%

commit v1 on v0

--- a/solution.py
+++ b/solution.py
@@ -1,6 +1,10 @@
+import functools
+
 import jax
 import jax.numpy as jnp
 from jax import lax
+from jax.experimental import pallas as pl
+from jax.experimental.pallas import tpu as pltpu
 from jax.sharding import PartitionSpec as P
 
 
@@ -160,6 +164,324 @@
     return (leaf_x, upper_x)
 
 
+def nt(left, right):
+    return lax.dot_general(
+        left, right, (((1,), (1,)), ((), ())), preferred_element_type=jnp.float32
+    )
+
+
+def nn(left, right):
+    return jnp.dot(left, right, preferred_element_type=jnp.float32)
+
+
+def tree_kernel(
+    n,
+    leaf_widths,
+    upper_widths,
+    leaf_rhs,
+    upper_rhs,
+    leaf_inv_h,
+    upper_inv_h,
+    leaf_panels_h,
+    mid_panels_h,
+    top_panels_h,
+    leaf_out,
+    upper_out,
+    leaf_inv,
+    upper_inv,
+    leaf_panels,
+    mid_panels,
+    top_panel,
+    r_full,
+    y_full,
+    root_full,
+    part_c,
+    part_s,
+    recv_c,
+    recv_s,
+    accum,
+    mine,
+    theirs,
+    load_sem,
+    send_sem,
+    recv_sem,
+    cross_send,
+    cross_recv,
+):
+    g = lax.axis_index("subtree")
+    p = lax.axis_index("panel")
+    rows = leaf_inv.shape[1]
+    far = n // 2
+    chip, core = p // 2, p % 2
+    steps = list(range(2, n)) + [1]
+
+    def ahead(k):
+        return ((chip + k // 2) % far) * 2 + (core + k % 2) % 2
+
+    def behind(k):
+        return ((chip + far - k // 2) % far) * 2 + (core + k % 2) % 2
+
+    def cols(index):
+        return pl.ds(pl.multiple_of(index * rows, rows), rows)
+
+    own = cols(p)
+
+    barrier = pltpu.get_barrier_semaphore()
+    for k in range(1, n):
+        pl.semaphore_signal(barrier, inc=1, device_id={"panel": ahead(k)})
+    for k in range(n):
+        pl.semaphore_signal(barrier, inc=1, device_id={"subtree": 1 - g, "panel": ahead(k)})
+
+    loads = {}
+
+    def load(key, src, dst):
+        loads[key] = pltpu.make_async_copy(src, dst, load_sem.at[len(loads)])
+        loads[key].start()
+
+    for s in range(4):
+        load(("inv", s), leaf_inv_h.at[s], leaf_inv.at[s])
+    for s in range(4):
+        load(("pan", s), leaf_panels_h.at[s], leaf_panels.at[s])
+    for i in range(2):
+        load(("inv", 4 + i), upper_inv_h.at[2 * g + i], upper_inv.at[i])
+    for i in range(2):
+        load(("pan", 4 + i), mid_panels_h.at[2 * g + i], mid_panels.at[i])
+    load(("inv", 6), upper_inv_h.at[4 + g], upper_inv.at[2])
+    load(("pan", 6), top_panels_h.at[g], top_panel)
+    load(("inv", 7), upper_inv_h.at[6], upper_inv.at[3])
+
+    def inverse(s):
+        return leaf_inv[s] if s < 4 else upper_inv[s - 4]
+
+    upper_index = {4: 2 * g, 5: 2 * g + 1, 6: 4 + g, 7: 6}
+    row_id = lax.broadcasted_iota(jnp.int32, (1, rows), 1) + p * rows
+
+    def masked(s, value):
+        width = leaf_widths[s] if s < 4 else upper_widths[upper_index[s]]
+        return jnp.where(row_id < width, value, 0.0)
+
+    pending = []
+
+    def send(src, dst, ssem, rsem, device):
+        copy = pltpu.make_async_remote_copy(
+            src_ref=src, dst_ref=dst, send_sem=ssem, recv_sem=rsem, device_id=device
+        )
+        copy.start()
+        pending.append(copy)
+
+    def arrived(dst, ssem, rsem):
+        pltpu.make_async_remote_copy(
+            src_ref=dst, dst_ref=dst, send_sem=ssem, recv_sem=rsem, device_id={"panel": ahead(1)}
+        ).wait_recv()
+
+    def gather_start(e, full, s, value):
+        full[s, :, own] = value
+        for k in steps:
+            block = full.at[s, :, own]
+            send(block, block, send_sem.at[e, s, k - 1], recv_sem.at[e, s, k - 1], {"panel": ahead(k)})
+
+    def gather_wait(e, full, s):
+        for k in reversed(steps):
+            arrived(full.at[s, :, cols(behind(k))], send_sem.at[e, s, k - 1], recv_sem.at[e, s, k - 1])
+        return full[s]
+
+    def scatter_start(e, part, recv, s, value):
+        part[s] = value.astype(jnp.bfloat16)
+        for k in steps:
+            send(
+                part.at[s, :, cols(ahead(k))],
+                recv.at[s, k - 1],
+                send_sem.at[e, s, k - 1],
+                recv_sem.at[e, s, k - 1],
+                {"panel": ahead(k)},
+            )
+
+    def scatter_wait(e, part, recv, s):
+        total = part[s, :, own].astype(jnp.float32)
+        for k in reversed(steps):
+            arrived(recv.at[s, k - 1], send_sem.at[e, s, k - 1], recv_sem.at[e, s, k - 1])
+            total = total + recv[s, k - 1].astype(jnp.float32)
+        return total
+
+    rhs_masked = [masked(s, leaf_rhs[s].astype(jnp.float32)).astype(jnp.bfloat16) for s in range(4)]
+    pl.semaphore_wait(barrier, 2 * n - 1)
+    for s in range(4):
+        gather_start(0, r_full, s, rhs_masked[s])
+
+    def solve_y(s):
+        full = gather_wait(0, r_full, s)
+        loads[("inv", s)].wait()
+        result = masked(s, nt(full, inverse(s))).astype(jnp.bfloat16)
+        gather_start(1, y_full, s, result)
+
+    def reduce_rhs(s, coupled):
+        value = (upper_rhs[upper_index[s]].astype(jnp.float32) - coupled).astype(jnp.bfloat16)
+        gather_start(0, r_full, s, masked(s, value.astype(jnp.float32)).astype(jnp.bfloat16))
+
+    for s in range(4):
+        solve_y(s)
+    to_mid = []
+    for s in range(4):
+        full = gather_wait(1, y_full, s)
+        loads[("pan", s)].wait()
+        to_mid.append(nt(full, leaf_panels[s, 0]))
+        if s % 2 == 1:
+            reduce_rhs(4 + s // 2, to_mid[s - 1] + to_mid[s])
+    to_high = nt(y_full[0], leaf_panels[0, 1])
+    for s in range(1, 4):
+        to_high = to_high + nt(y_full[s], leaf_panels[s, 1])
+    solve_y(4)
+    solve_y(5)
+    to_root = nt(y_full[0], leaf_panels[0, 2])
+    for s in range(1, 4):
+        to_root = to_root + nt(y_full[s], leaf_panels[s, 2])
+    for s in (4, 5):
+        full = gather_wait(1, y_full, s)
+        loads[("pan", s)].wait()
+        to_high = to_high + nt(full, mid_panels[s - 4, 0])
+    reduce_rhs(6, to_high)
+    for s in (4, 5):
+        to_root = to_root + nt(y_full[s], mid_panels[s - 4, 1])
+    solve_y(6)
+    full = gather_wait(1, y_full, 6)
+    loads[("pan", 6)].wait()
+    to_root = to_root + nt(full, top_panel[...])
+
+    base = jnp.where(g == 0, upper_rhs[6].astype(jnp.float32), 0.0)
+    root_full[g, :, own] = masked(7, base - to_root).astype(jnp.bfloat16)
+    block = root_full.at[g, :, own]
+    for k in steps + [0]:
+        send(
+            block,
+            block,
+            cross_send.at[k],
+            cross_recv.at[k],
+            {"subtree": 1 - g, "panel": ahead(k)},
+        )
+        if k > 0:
+            send(block, block, send_sem.at[0, 7, k - 1], recv_sem.at[0, 7, k - 1], {"panel": ahead(k)})
+    loads[("inv", 7)].wait()
+    for k in reversed(steps):
+        arrived(
+            root_full.at[g, :, cols(behind(k))], send_sem.at[0, 7, k - 1], recv_sem.at[0, 7, k - 1]
+        )
+    for k in [0] + steps:
+        arrived(root_full.at[1 - g, :, cols(behind(k))], cross_send.at[k], cross_recv.at[k])
+    reduced = (root_full[0].astype(jnp.float32) + root_full[1].astype(jnp.float32)).astype(jnp.bfloat16)
+    lifted = masked(7, nt(reduced, inverse(7))).astype(jnp.bfloat16)
+
+    def lift(s):
+        own_y = y_full[s, :, own].astype(jnp.float32)
+        value = (own_y - scatter_wait(2, part_c, recv_c, s)).astype(jnp.bfloat16)
+        value = masked(s, value.astype(jnp.float32)).astype(jnp.bfloat16)
+        scatter_start(3, part_s, recv_s, s, nn(value, inverse(s)))
+
+    def solved(s):
+        return masked(s, scatter_wait(3, part_s, recv_s, s)).astype(jnp.bfloat16)
+
+    scatter_start(3, part_s, recv_s, 7, nn(lifted, inverse(7)))
+    root_x = solved(7)
+    scatter_start(2, part_c, recv_c, 6, nn(root_x, top_panel[...]))
+    upper_out[6] = root_x
+    for i in range(2):
+        accum[4 + i] = nn(root_x, mid_panels[i, 1])
+    lift(6)
+    for s in range(4):
+        accum[s] = nn(root_x, leaf_panels[s, 2])
+    high_x = solved(6)
+    for s in (4, 5):
+        scatter_start(2, part_c, recv_c, s, accum[s] + nn(high_x, mid_panels[s - 4, 0]))
+
+    def share(i, s, value):
+        upper_out[upper_index[s]] = value
+        mine[i] = value
+        send(mine.at[i], theirs.at[i], cross_send.at[n + i], cross_recv.at[n + i], {"subtree": 1 - g})
+
+    share(2, 6, high_x)
+    for s in range(4):
+        accum[s] = accum[s] + nn(high_x, leaf_panels[s, 1])
+    lift(4)
+    lift(5)
+    for i in range(2):
+        mid_x = solved(4 + i)
+        for s in (2 * i, 2 * i + 1):
+            scatter_start(2, part_c, recv_c, s, accum[s] + nn(mid_x, leaf_panels[s, 0]))
+        share(i, 4 + i, mid_x)
+    for s in range(4):
+        lift(s)
+    for i, slot in ((0, 2 * (1 - g)), (1, 2 * (1 - g) + 1), (2, 5 - g)):
+        arrived(theirs.at[i], cross_send.at[n + i], cross_recv.at[n + i])
+        upper_out[slot] = theirs[i]
+    for s in range(4):
+        leaf_out[s] = solved(s)
+    for copy in pending:
+        copy.wait_send()
+
+
+def half_tree(
+    n,
+    leaf_rhs,
+    upper_rhs,
+    leaf_inv,
+    upper_inv,
+    leaf_panels,
+    mid_panels,
+    top_panels,
+    leaf_widths,
+    upper_widths,
+):
+    rows, width, count = leaf_inv.shape[1], leaf_inv.shape[2], leaf_rhs.shape[2]
+    low = jnp.bfloat16
+    smem = pl.BlockSpec(memory_space=pltpu.SMEM)
+    vmem = pl.BlockSpec(memory_space=pltpu.VMEM)
+    hbm = pl.BlockSpec(memory_space=pltpu.HBM)
+    leaf_t, upper_t = pl.pallas_call(
+        functools.partial(tree_kernel, n),
+        out_shape=[
+            jax.ShapeDtypeStruct((4, count, rows), low),
+            jax.ShapeDtypeStruct((7, count, rows), low),
+        ],
+        in_specs=[smem, smem, vmem, vmem, hbm, hbm, hbm, hbm, hbm],
+        out_specs=[vmem, vmem],
+        scratch_shapes=[
+            pltpu.VMEM((4, rows, width), low),
+            pltpu.VMEM((4, rows, width), low),
+            pltpu.VMEM((4, 3, rows, width), low),
+            pltpu.VMEM((2, 2, rows, width), low),
+            pltpu.VMEM((rows, width), low),
+            pltpu.VMEM((7, count, width), low),
+            pltpu.VMEM((7, count, width), low),
+            pltpu.VMEM((2, count, width), low),
+            pltpu.VMEM((7, count, width), low),
+            pltpu.VMEM((8, count, width), low),
+            pltpu.VMEM((7, n - 1, count, rows), low),
+            pltpu.VMEM((8, n - 1, count, rows), low),
+            pltpu.VMEM((6, count, width), jnp.float32),
+            pltpu.VMEM((3, count, rows), low),
+            pltpu.VMEM((3, count, rows), low),
+            pltpu.SemaphoreType.DMA((15,)),
+            pltpu.SemaphoreType.DMA((4, 8, n - 1)),
+            pltpu.SemaphoreType.DMA((4, 8, n - 1)),
+            pltpu.SemaphoreType.DMA((n + 3,)),
+            pltpu.SemaphoreType.DMA((n + 3,)),
+        ],
+        compiler_params=pltpu.CompilerParams(
+            collective_id=0, has_side_effects=True, vmem_limit_bytes=48 * 1024 * 1024
+        ),
+    )(
+        leaf_widths,
+        upper_widths,
+        jnp.swapaxes(leaf_rhs, 1, 2),
+        jnp.swapaxes(upper_rhs, 1, 2),
+        leaf_inv,
+        upper_inv,
+        leaf_panels,
+        mid_panels,
+        top_panels,
+    )
+    return jnp.swapaxes(leaf_t, 1, 2), jnp.swapaxes(upper_t, 1, 2)
+
+
 def solution(mesh):
     in_specs = (
         P("subtree", "panel", "snap"),
@@ -173,6 +495,11 @@
         P(),
     )
     out_specs = (P("subtree", "panel", "snap"), P(None, "panel", "snap"))
+    panel_count = mesh.shape["panel"]
+    if mesh.shape["subtree"] == 2 and panel_count % 2 == 0:
+        body = functools.partial(half_tree, panel_count)
+    else:
+        body = per_device
     return jax.shard_map(
-        per_device, mesh=mesh, in_specs=in_specs, out_specs=out_specs, check_vma=False
-    )
+        body, mesh=mesh, in_specs=in_specs, out_specs=out_specs, check_vma=False
+    )

time: 255 us -> 62.7 us (0.25)
  waiting for transfers between devices: 151 us -> 0 us
  Pallas kernels: 0 us -> 54.6 us
  blocking collectives: 44.9 us -> 0 us
  matrix products: 35.5 us -> 0 us
  between operations: 14.5 us -> 0.66 us
  local copies, waits for them, and re-layouts: 1.02 us -> 7.13 us
  other arithmetic: 6.07 us -> 0 us
    reduce_scatter x8 -> x0, waiting for transfers between devices: 151 us -> none  [the longest x4 79.6 us: solve_up(): lax.psum_scatter(jnp.einsum('nrw,nrc->wnc', inverse, masked, preferred_el...]
    pallas_call x0 -> x1, Pallas kernels: none -> 54.6 us  [half_tree(): pl.pallas_call(functools.partial(tree_kernel, n), out_shape=[jax.ShapeDty...]
    all_gather x8 -> x0, blocking collectives: 44.9 us -> none  [the longest x4 23.4 us: solve_down(): lax.all_gather(reduced, 'panel', axis=1, tiled=True) * live_cols[:, :, None]]
    dot_general x25 -> x0, matrix products: 35.5 us -> none  [the longest x4 9.13 us: solve_up(): jnp.einsum('nrw,nrc->wnc', inverse, masked, preferred_element_type=jnp.fl...]
    unnamed x13 -> x14, local copies, waits for them, and re-layouts: 0.69 us -> 7.13 us
    convert_element_type x14 -> x0, other arithmetic: 5.59 us -> none  [the longest x4 3.67 us: solve_up(): (jnp.transpose(summed, (1, 0, 2)) * own_live[:, :, None]).astype(jnp.bflo...]
  transfers between devices with their start and end apart: 8 -> 0, of which waited for: 8 -> 0; matrix products, arithmetic and copies ran while one was open for 0% -> 0% of each run, Pallas kernels for 0% -> 0%
where the time goes in v1:
time: 62.7 us; the launch traced here: 62.4 us
  Pallas kernels  54.6 us (87%)
  local copies, waits for them, and re-layouts  7.13 us (11%)
  between operations  0.66 us (1%)
    pallas_call x1, Pallas kernels, half_tree(): pl.pallas_call(functools.partial(tree_kernel, n), out_shape=[jax.ShapeDty...  54.6 us
    unnamed x14, local copies, waits for them, and re-layouts  7.13 us

profile of v1, /device:TPU:0, one launch (start us, length us, event | category | flops | bytes accessed | tf_op | source)
XLA Modules:
  0.0 62.4 jit_solution(6167419906250272168)
XLA Ops:
  0.6 0.0 copy-start
  0.6 1.6 %copy-done = bf16[4,256,1024]{2,1,0:T(8,128)(2,1)S(1)} copy-done((bf16[4,256,1024]{2,1,0:T(8,128)(2,1)S(1)}, bf16[4,256,1024]{2,1,0:T(8,128)(2,1)}, u32[]{:S(2)}) %copy-start) | copy-done | bytes 2097176
  2.2 0.0 copy-start.1
  2.2 1.2 %copy-done.1 = bf16[2,256,1024]{2,1,0:T(8,128)(2,1)S(1)} copy-done((bf16[2,256,1024]{2,1,0:T(8,128)(2,1)S(1)}, bf16[2,256,1024]{2,1,0:T(8,128)(2,1)}, u32[]{:S(2)}) %copy-start.1) | copy-done | bytes 1048600
  3.5 0.0 copy-start.2
  3.5 0.9 %copy-done.2 = bf16[7,256,32]{1,2,0:T(8,128)(2,1)S(1)} copy-done((bf16[7,256,32]{1,2,0:T(8,128)(2,1)S(1)}, bf16[7,256,32]{1,2,0:T(8,128)(2,1)}, u32[]{:S(2)}) %copy-start.2) | copy-done | bytes 114712
  4.3 0.0 copy-start.3
  4.4 0.8 %copy-done.3 = bf16[4,256,32]{1,2,0:T(8,128)(2,1)S(1)} copy-done((bf16[4,256,32]{1,2,0:T(8,128)(2,1)S(1)}, bf16[4,256,32]{1,2,0:T(8,128)(2,1)}, u32[]{:S(2)}) %copy-start.3) | copy-done | bytes 65560
  5.2 0.0 copy-start.4
  5.2 0.7 %copy-done.4 = s32[4]{0:T(128)S(1)} copy-done((s32[4]{0:T(128)S(1)}, s32[4]{0:T(128)}, u32[]{:S(2)}) %copy-start.4) | copy-done | bytes 40
  5.8 0.0 copy-start.5
  5.8 0.7 %copy-done.5 = s32[7]{0:T(128)S(1)} copy-done((s32[7]{0:T(128)S(1)}, s32[7]{0:T(128)}, u32[]{:S(2)}) %copy-start.5) | copy-done | bytes 52
  6.5 54.6 %shard_map.104 = (bf16[4,32,256]{2,1,0:T(8,128)(2,1)S(1)}, bf16[7,32,256]{2,1,0:T(8,128)(2,1)S(1)}) custom-call(s32[4]{0:T(128)S(1)} %copy-done.4, s32[7]{0:T(128)S(1)} %copy-done.5, bf16[4,32,256]{2,1,0:T(8,128)(2,1)S(1)} %bitcast.6, bf16[7,32,256]{2,1,0:T(8,128)(2,1)S(1)} %bitcast.4, bf16[4,256,1024]{2,1,0:T(8,128)(2,1)S(1)} %copy-done, ...), custom_call_target="tpu_custom_call" | custom-call | tf_op jit(solution)/shard_map/pallas_call | solution.py:438
  61.1 0.6 %copy.13 = bf16[4,256,32]{1,2,0:T(8,128)(2,1)} copy(bf16[4,256,32]{1,2,0:T(8,128)(2,1)S(1)} %bitcast.7) | data formatting | bytes 131072
  61.8 0.6 %copy.14 = bf16[7,256,32]{1,2,0:T(8,128)(2,1)} copy(bf16[7,256,32]{1,2,0:T(8,128)(2,1)S(1)} %bitcast.5) | data formatting | bytes 229376
Async XLA Ops:
  0.6 1.6 %copy-start = (bf16[4,256,1024]{2,1,0:T(8,128)(2,1)S(1)}, bf16[4,256,1024]{2,1,0:T(8,128)(2,1)}, u32[]{:S(2)}) copy-start(bf16[4,256,1024]{2,1,0:T(8,128)(2,1)} %leaf_inv_h.1) | copy-start | bytes 6291460
  2.2 1.2 %copy-start.1 = (bf16[2,256,1024]{2,1,0:T(8,128)(2,1)S(1)}, bf16[2,256,1024]{2,1,0:T(8,128)(2,1)}, u32[]{:S(2)}) copy-start(bf16[2,256,1024]{2,1,0:T(8,128)(2,1)} %top_panels_h.1) | copy-start | bytes 3145732
  3.5 0.9 %copy-start.2 = (bf16[7,256,32]{1,2,0:T(8,128)(2,1)S(1)}, bf16[7,256,32]{1,2,0:T(8,128)(2,1)}, u32[]{:S(2)}) copy-start(bf16[7,256,32]{1,2,0:T(8,128)(2,1)} %param.10) | copy-start | bytes 344068
  4.3 0.8 %copy-start.3 = (bf16[4,256,32]{1,2,0:T(8,128)(2,1)S(1)}, bf16[4,256,32]{1,2,0:T(8,128)(2,1)}, u32[]{:S(2)}) copy-start(bf16[4,256,32]{1,2,0:T(8,128)(2,1)} %param.9) | copy-start | bytes 196612
  5.2 0.7 %copy-start.4 = (s32[4]{0:T(128)S(1)}, s32[4]{0:T(128)}, u32[]{:S(2)}) copy-start(s32[4]{0:T(128)} %leaf_widths.1) | copy-start | bytes 52
  5.8 0.7 %copy-start.5 = (s32[7]{0:T(128)S(1)}, s32[7]{0:T(128)}, u32[]{:S(2)}) copy-start(s32[7]{0:T(128)} %upper_widths.1) | copy-start | bytes 88

commit v2 on v1

--- a/solution.py
+++ b/solution.py
@@ -176,17 +176,21 @@
 
 def tree_kernel(
     n,
-    leaf_widths,
-    upper_widths,
-    leaf_rhs,
-    upper_rhs,
+    leaf_widths_h,
+    upper_widths_h,
+    leaf_rhs_h,
+    upper_rhs_h,
     leaf_inv_h,
     upper_inv_h,
     leaf_panels_h,
     mid_panels_h,
     top_panels_h,
-    leaf_out,
-    upper_out,
+    leaf_out_h,
+    upper_out_h,
+    leaf_widths,
+    upper_widths,
+    leaf_rhs,
+    upper_rhs,
     leaf_inv,
     upper_inv,
     leaf_panels,
@@ -202,11 +206,14 @@
     accum,
     mine,
     theirs,
+    leaf_out,
+    root_out,
     load_sem,
     send_sem,
     recv_sem,
     cross_send,
     cross_recv,
+    store_sem,
 ):
     g = lax.axis_index("subtree")
     p = lax.axis_index("panel")
@@ -232,14 +239,24 @@
     for k in range(n):
         pl.semaphore_signal(barrier, inc=1, device_id={"subtree": 1 - g, "panel": ahead(k)})
 
+    stores = []
+
+    def store(src, dst):
+        stores.append(pltpu.make_async_copy(src, dst, store_sem.at[len(stores)]))
+        stores[-1].start()
+
     loads = {}
 
     def load(key, src, dst):
         loads[key] = pltpu.make_async_copy(src, dst, load_sem.at[len(loads)])
         loads[key].start()
 
+    load("leaf_rhs", leaf_rhs_h, leaf_rhs)
+    load("leaf_widths", leaf_widths_h, leaf_widths)
+    load("upper_widths", upper_widths_h, upper_widths)
     for s in range(4):
         load(("inv", s), leaf_inv_h.at[s], leaf_inv.at[s])
+    load("upper_rhs", upper_rhs_h, upper_rhs)
     for s in range(4):
         load(("pan", s), leaf_panels_h.at[s], leaf_panels.at[s])
     for i in range(2):
@@ -303,6 +320,8 @@
             total = total + recv[s, k - 1].astype(jnp.float32)
         return total
 
+    for key in ("leaf_rhs", "leaf_widths", "upper_widths"):
+        loads[key].wait()
     rhs_masked = [masked(s, leaf_rhs[s].astype(jnp.float32)).astype(jnp.bfloat16) for s in range(4)]
     pl.semaphore_wait(barrier, 2 * n - 1)
     for s in range(4):
@@ -320,6 +339,7 @@
 
     for s in range(4):
         solve_y(s)
+    loads["upper_rhs"].wait()
     to_mid = []
     for s in range(4):
         full = gather_wait(1, y_full, s)
@@ -382,7 +402,8 @@
     scatter_start(3, part_s, recv_s, 7, nn(lifted, inverse(7)))
     root_x = solved(7)
     scatter_start(2, part_c, recv_c, 6, nn(root_x, top_panel[...]))
-    upper_out[6] = root_x
+    root_out[...] = root_x
+    store(root_out, upper_out_h.at[6])
     for i in range(2):
         accum[4 + i] = nn(root_x, mid_panels[i, 1])
     lift(6)
@@ -393,8 +414,8 @@
         scatter_start(2, part_c, recv_c, s, accum[s] + nn(high_x, mid_panels[s - 4, 0]))
 
     def share(i, s, value):
-        upper_out[upper_index[s]] = value
         mine[i] = value
+        store(mine.at[i], upper_out_h.at[upper_index[s]])
         send(mine.at[i], theirs.at[i], cross_send.at[n + i], cross_recv.at[n + i], {"subtree": 1 - g})
 
     share(2, 6, high_x)
@@ -411,11 +432,14 @@
         lift(s)
     for i, slot in ((0, 2 * (1 - g)), (1, 2 * (1 - g) + 1), (2, 5 - g)):
         arrived(theirs.at[i], cross_send.at[n + i], cross_recv.at[n + i])
-        upper_out[slot] = theirs[i]
+        store(theirs.at[i], upper_out_h.at[slot])
     for s in range(4):
         leaf_out[s] = solved(s)
+        store(leaf_out.at[s], leaf_out_h.at[s])
     for copy in pending:
         copy.wait_send()
+    for copy in stores:
+        copy.wait()
 
 
 def half_tree(
@@ -432,8 +456,6 @@
 ):
     rows, width, count = leaf_inv.shape[1], leaf_inv.shape[2], leaf_rhs.shape[2]
     low = jnp.bfloat16
-    smem = pl.BlockSpec(memory_space=pltpu.SMEM)
-    vmem = pl.BlockSpec(memory_space=pltpu.VMEM)
     hbm = pl.BlockSpec(memory_space=pltpu.HBM)
     leaf_t, upper_t = pl.pallas_call(
         functools.partial(tree_kernel, n),
@@ -441,9 +463,13 @@
             jax.ShapeDtypeStruct((4, count, rows), low),
             jax.ShapeDtypeStruct((7, count, rows), low),
         ],
-        in_specs=[smem, smem, vmem, vmem, hbm, hbm, hbm, hbm, hbm],
-        out_specs=[vmem, vmem],
+        in_specs=[hbm] * 9,
+        out_specs=[hbm, hbm],
         scratch_shapes=[
+            pltpu.SMEM(leaf_widths.shape, jnp.int32),
+            pltpu.SMEM(upper_widths.shape, jnp.int32),
+            pltpu.VMEM((4, count, rows), low),
+            pltpu.VMEM((7, count, rows), low),
             pltpu.VMEM((4, rows, width), low),
             pltpu.VMEM((4, rows, width), low),
             pltpu.VMEM((4, 3, rows, width), low),
@@ -459,14 +485,17 @@
             pltpu.VMEM((6, count, width), jnp.float32),
             pltpu.VMEM((3, count, rows), low),
             pltpu.VMEM((3, count, rows), low),
-            pltpu.SemaphoreType.DMA((15,)),
+            pltpu.VMEM((4, count, rows), low),
+            pltpu.VMEM((count, rows), low),
+            pltpu.SemaphoreType.DMA((19,)),
             pltpu.SemaphoreType.DMA((4, 8, n - 1)),
             pltpu.SemaphoreType.DMA((4, 8, n - 1)),
             pltpu.SemaphoreType.DMA((n + 3,)),
             pltpu.SemaphoreType.DMA((n + 3,)),
+            pltpu.SemaphoreType.DMA((11,)),
         ],
         compiler_params=pltpu.CompilerParams(
-            collective_id=0, has_side_effects=True, vmem_limit_bytes=48 * 1024 * 1024
+            collective_id=0, has_side_effects=True, vmem_limit_bytes=58 * 1024 * 1024
         ),
     )(
         leaf_widths,

time: 62.7 us -> 58.5 us (0.933)
  local copies, waits for them, and re-layouts: 7.13 us -> 3.02 us
    unnamed x14 -> x2, local copies, waits for them, and re-layouts: 7.13 us -> 3.02 us
where the time goes in v2:
time: 58.5 us; the launch traced here: 58.3 us
  Pallas kernels  54.7 us (94%)
  local copies, waits for them, and re-layouts  3.02 us (5%)
  between operations  0.64 us (1%)
    pallas_call x1, Pallas kernels, half_tree(): pl.pallas_call(functools.partial(tree_kernel, n), out_shape=[jax.ShapeDty...  54.7 us
    unnamed x2, local copies, waits for them, and re-layouts  3.02 us

profile of v2, /device:TPU:0, one launch (start us, length us, event | category | flops | bytes accessed | tf_op | source)
XLA Modules:
  0.0 58.3 jit_solution(12479616107565513632)
XLA Ops:
  0.6 54.7 %shard_map.104 = (bf16[4,32,256]{2,1,0:T(8,128)(2,1)}, bf16[7,32,256]{2,1,0:T(8,128)(2,1)}) custom-call(s32[4]{0:T(128)} %leaf_widths_h.1, s32[7]{0:T(128)} %upper_widths_h.1, bf16[4,32,256]{2,1,0:T(8,128)(2,1)} %bitcast.6, bf16[7,32,256]{2,1,0:T(8,128)(2,1)} %bitcast.4, bf16[4,256,1024]{2,1,0:T(8,128)(2,1)} %leaf_inv_h.1, ...), custom_call_target="tpu_custom_call" | custom-call | tf_op jit(solution)/shard_map/pallas_call | solution.py:460
  55.3 1.5 %copy.13 = bf16[4,256,32]{1,2,0:T(8,128)(2,1)} copy(bf16[4,256,32]{1,2,0:T(8,128)(2,1)} %bitcast.7) | data formatting | bytes 131072
  56.8 1.6 %copy.14 = bf16[7,256,32]{1,2,0:T(8,128)(2,1)} copy(bf16[7,256,32]{1,2,0:T(8,128)(2,1)} %bitcast.5) | data formatting | bytes 229376

commit v3 on v2

--- a/solution.py
+++ b/solution.py
@@ -207,7 +207,7 @@
     mine,
     theirs,
     leaf_out,
-    root_out,
+    sep_out,
     load_sem,
     send_sem,
     recv_sem,
@@ -402,8 +402,8 @@
     scatter_start(3, part_s, recv_s, 7, nn(lifted, inverse(7)))
     root_x = solved(7)
     scatter_start(2, part_c, recv_c, 6, nn(root_x, top_panel[...]))
-    root_out[...] = root_x
-    store(root_out, upper_out_h.at[6])
+    sep_out[6] = root_x.astype(jnp.float32)
+    store(sep_out.at[6], upper_out_h.at[6])
     for i in range(2):
         accum[4 + i] = nn(root_x, mid_panels[i, 1])
     lift(6)
@@ -415,7 +415,8 @@
 
     def share(i, s, value):
         mine[i] = value
-        store(mine.at[i], upper_out_h.at[upper_index[s]])
+        sep_out[i] = value.astype(jnp.float32)
+        store(sep_out.at[i], upper_out_h.at[upper_index[s]])
         send(mine.at[i], theirs.at[i], cross_send.at[n + i], cross_recv.at[n + i], {"subtree": 1 - g})
 
     share(2, 6, high_x)
@@ -432,9 +433,10 @@
         lift(s)
     for i, slot in ((0, 2 * (1 - g)), (1, 2 * (1 - g) + 1), (2, 5 - g)):
         arrived(theirs.at[i], cross_send.at[n + i], cross_recv.at[n + i])
-        store(theirs.at[i], upper_out_h.at[slot])
-    for s in range(4):
-        leaf_out[s] = solved(s)
+        sep_out[3 + i] = theirs[i].astype(jnp.float32)
+        store(sep_out.at[3 + i], upper_out_h.at[slot])
+    for s in range(4):
+        leaf_out[s] = masked(s, scatter_wait(3, part_s, recv_s, s))
         store(leaf_out.at[s], leaf_out_h.at[s])
     for copy in pending:
         copy.wait_send()
@@ -460,8 +462,8 @@
     leaf_t, upper_t = pl.pallas_call(
         functools.partial(tree_kernel, n),
         out_shape=[
-            jax.ShapeDtypeStruct((4, count, rows), low),
-            jax.ShapeDtypeStruct((7, count, rows), low),
+            jax.ShapeDtypeStruct((4, count, rows), jnp.float32),
+            jax.ShapeDtypeStruct((7, count, rows), jnp.float32),
         ],
         in_specs=[hbm] * 9,
         out_specs=[hbm, hbm],
@@ -485,8 +487,8 @@
             pltpu.VMEM((6, count, width), jnp.float32),
             pltpu.VMEM((3, count, rows), low),
             pltpu.VMEM((3, count, rows), low),
-            pltpu.VMEM((4, count, rows), low),
-            pltpu.VMEM((count, rows), low),
+            pltpu.VMEM((4, count, rows), jnp.float32),
+            pltpu.VMEM((7, count, rows), jnp.float32),
             pltpu.SemaphoreType.DMA((19,)),
             pltpu.SemaphoreType.DMA((4, 8, n - 1)),
             pltpu.SemaphoreType.DMA((4, 8, n - 1)),
@@ -508,7 +510,7 @@
         mid_panels,
         top_panels,
     )
-    return jnp.swapaxes(leaf_t, 1, 2), jnp.swapaxes(upper_t, 1, 2)
+    return jnp.swapaxes(leaf_t.astype(low), 1, 2), jnp.swapaxes(upper_t.astype(low), 1, 2)
 
 
 def solution(mesh):

time: 58.5 us -> 58.6 us (level)
  other arithmetic: 0 us -> 3.14 us
  local copies, waits for them, and re-layouts: 3.02 us -> 0 us
    transpose x0 -> x2, other arithmetic: none -> 3.14 us  [the longest x1 1.6 us: half_tree(): jnp.swapaxes(upper_t.astype(low), 1, 2)]
    unnamed x2 -> x0, local copies, waits for them, and re-layouts: 3.02 us -> none
where the time goes in v3:
time: 58.6 us; the launch traced here: 58.5 us
  Pallas kernels  54.7 us (93%)
  other arithmetic  3.14 us (5%)
  between operations  0.64 us (1%)
    pallas_call x1, Pallas kernels, half_tree(): pl.pallas_call(functools.partial(tree_kernel, n), out_shape=[jax.ShapeDty...  54.7 us
    transpose x1, other arithmetic, half_tree(): jnp.swapaxes(upper_t.astype(low), 1, 2)  1.6 us
    transpose x1, other arithmetic, half_tree(): jnp.swapaxes(leaf_t.astype(low), 1, 2)  1.54 us

profile of v3, /device:TPU:0, one launch (start us, length us, event | category | flops | bytes accessed | tf_op | source)
XLA Modules:
  0.0 58.5 jit_solution(2684223549420192542)
XLA Ops:
  0.6 54.7 %shard_map.104 = (f32[4,32,256]{2,1,0:T(8,128)}, f32[7,32,256]{2,1,0:T(8,128)}) custom-call(s32[4]{0:T(128)} %leaf_widths_h.1, s32[7]{0:T(128)} %upper_widths_h.1, bf16[4,32,256]{2,1,0:T(8,128)(2,1)} %bitcast.7, bf16[7,32,256]{2,1,0:T(8,128)(2,1)} %bitcast.6, bf16[4,256,1024]{2,1,0:T(8,128)(2,1)} %leaf_inv_h.1, bf16[7,256,1024]{2,1,0:T(8,128)(2,1)} %upper_inv_h.1, ...), custom_call_target="tpu_custom_call" | custom-call | tf_op jit(solution)/shard_map/pallas_call | solution.py:462
  55.3 1.5 %convert_bitcast_fusion.1 = bf16[4,256,32]{1,2,0:T(8,128)(2,1)} fusion(f32[4,32,256]{2,1,0:T(8,128)} %get-tuple-element.4), kind=kLoop, calls=%fused_computation.1 | loop fusion | flops 32768 | bytes 196608 | tf_op jit(solution)/shard_map/transpose | solution.py:513
  56.9 1.6 %convert_bitcast_fusion = bf16[7,256,32]{1,2,0:T(8,128)(2,1)} fusion(f32[7,32,256]{2,1,0:T(8,128)} %get-tuple-element.5), kind=kLoop, calls=%fused_computation | loop fusion | flops 57344 | bytes 344064 | tf_op jit(solution)/shard_map/transpose | solution.py:513

commit v4 on v2

--- a/solution.py
+++ b/solution.py
@@ -185,8 +185,8 @@
     leaf_panels_h,
     mid_panels_h,
     top_panels_h,
-    leaf_out_h,
-    upper_out_h,
+    leaf_out,
+    upper_out,
     leaf_widths,
     upper_widths,
     leaf_rhs,
@@ -206,14 +206,11 @@
     accum,
     mine,
     theirs,
-    leaf_out,
-    root_out,
     load_sem,
     send_sem,
     recv_sem,
     cross_send,
     cross_recv,
-    store_sem,
 ):
     g = lax.axis_index("subtree")
     p = lax.axis_index("panel")
@@ -238,12 +235,6 @@
         pl.semaphore_signal(barrier, inc=1, device_id={"panel": ahead(k)})
     for k in range(n):
         pl.semaphore_signal(barrier, inc=1, device_id={"subtree": 1 - g, "panel": ahead(k)})
-
-    stores = []
-
-    def store(src, dst):
-        stores.append(pltpu.make_async_copy(src, dst, store_sem.at[len(stores)]))
-        stores[-1].start()
 
     loads = {}
 
@@ -402,8 +393,7 @@
     scatter_start(3, part_s, recv_s, 7, nn(lifted, inverse(7)))
     root_x = solved(7)
     scatter_start(2, part_c, recv_c, 6, nn(root_x, top_panel[...]))
-    root_out[...] = root_x
-    store(root_out, upper_out_h.at[6])
+    upper_out[6] = root_x
     for i in range(2):
         accum[4 + i] = nn(root_x, mid_panels[i, 1])
     lift(6)
@@ -414,8 +404,8 @@
         scatter_start(2, part_c, recv_c, s, accum[s] + nn(high_x, mid_panels[s - 4, 0]))
 
     def share(i, s, value):
+        upper_out[upper_index[s]] = value
         mine[i] = value
-        store(mine.at[i], upper_out_h.at[upper_index[s]])
         send(mine.at[i], theirs.at[i], cross_send.at[n + i], cross_recv.at[n + i], {"subtree": 1 - g})
 
     share(2, 6, high_x)
@@ -432,14 +422,11 @@
         lift(s)
     for i, slot in ((0, 2 * (1 - g)), (1, 2 * (1 - g) + 1), (2, 5 - g)):
         arrived(theirs.at[i], cross_send.at[n + i], cross_recv.at[n + i])
-        store(theirs.at[i], upper_out_h.at[slot])
+        upper_out[slot] = theirs[i]
     for s in range(4):
         leaf_out[s] = solved(s)
-        store(leaf_out.at[s], leaf_out_h.at[s])
     for copy in pending:
         copy.wait_send()
-    for copy in stores:
-        copy.wait()
 
 
 def half_tree(
@@ -456,6 +443,7 @@
 ):
     rows, width, count = leaf_inv.shape[1], leaf_inv.shape[2], leaf_rhs.shape[2]
     low = jnp.bfloat16
+    vmem = pl.BlockSpec(memory_space=pltpu.VMEM)
     hbm = pl.BlockSpec(memory_space=pltpu.HBM)
     leaf_t, upper_t = pl.pallas_call(
         functools.partial(tree_kernel, n),
@@ -464,7 +452,7 @@
             jax.ShapeDtypeStruct((7, count, rows), low),
         ],
         in_specs=[hbm] * 9,
-        out_specs=[hbm, hbm],
+        out_specs=[vmem, vmem],
         scratch_shapes=[
             pltpu.SMEM(leaf_widths.shape, jnp.int32),
             pltpu.SMEM(upper_widths.shape, jnp.int32),
@@ -485,17 +473,14 @@
             pltpu.VMEM((6, count, width), jnp.float32),
             pltpu.VMEM((3, count, rows), low),
             pltpu.VMEM((3, count, rows), low),
-            pltpu.VMEM((4, count, rows), low),
-            pltpu.VMEM((count, rows), low),
             pltpu.SemaphoreType.DMA((19,)),
             pltpu.SemaphoreType.DMA((4, 8, n - 1)),
             pltpu.SemaphoreType.DMA((4, 8, n - 1)),
             pltpu.SemaphoreType.DMA((n + 3,)),
             pltpu.SemaphoreType.DMA((n + 3,)),
-            pltpu.SemaphoreType.DMA((11,)),
         ],
         compiler_params=pltpu.CompilerParams(
-            collective_id=0, has_side_effects=True, vmem_limit_bytes=58 * 1024 * 1024
+            collective_id=0, has_side_effects=True, vmem_limit_bytes=(53 * 1024 + 736) * 1024
         ),
     )(
         leaf_widths,

time: 58.5 us -> 59.9 us (1.024)
  local copies, waits for them, and re-layouts: 3.02 us -> 4.32 us
    unnamed x2 -> x8, local copies, waits for them, and re-layouts: 3.02 us -> 4.32 us
where the time goes in v4:
time: 59.9 us; the launch traced here: 59.7 us
  Pallas kernels  54.7 us (91%)
  local copies, waits for them, and re-layouts  4.32 us (7%)
  between operations  0.65 us (1%)
    pallas_call x1, Pallas kernels, half_tree(): pl.pallas_call(functools.partial(tree_kernel, n), out_shape=[jax.ShapeDty...  54.7 us
    unnamed x8, local copies, waits for them, and re-layouts  4.32 us

profile of v4, /device:TPU:0, one launch (start us, length us, event | category | flops | bytes accessed | tf_op | source)
XLA Modules:
  0.0 59.7 jit_solution(9279185614499405623)
XLA Ops:
  0.6 0.0 copy-start
  0.6 0.8 %copy-done = bf16[4,256,32]{1,2,0:T(8,128)(2,1)S(1)} copy-done((bf16[4,256,32]{1,2,0:T(8,128)(2,1)S(1)}, bf16[4,256,32]{1,2,0:T(8,128)(2,1)}, u32[]{:S(2)}) %copy-start) | copy-done | bytes 65560
  1.5 0.0 copy-start.1
  1.5 0.7 %copy-done.1 = s32[4]{0:T(128)S(1)} copy-done((s32[4]{0:T(128)S(1)}, s32[4]{0:T(128)}, u32[]{:S(2)}) %copy-start.1) | copy-done | bytes 40
  2.1 0.0 copy-start.2
  2.1 0.7 %copy-done.2 = s32[7]{0:T(128)S(1)} copy-done((s32[7]{0:T(128)S(1)}, s32[7]{0:T(128)}, u32[]{:S(2)}) %copy-start.2) | copy-done | bytes 52
  2.8 54.7 %shard_map.104 = (bf16[4,32,256]{2,1,0:T(8,128)(2,1)S(1)}, bf16[7,32,256]{2,1,0:T(8,128)(2,1)}) custom-call(s32[4]{0:T(128)S(1)} %copy-done.1, s32[7]{0:T(128)S(1)} %copy-done.2, bf16[4,32,256]{2,1,0:T(8,128)(2,1)S(1)} %bitcast.4, bf16[7,32,256]{2,1,0:T(8,128)(2,1)} %bitcast.6, bf16[4,256,1024]{2,1,0:T(8,128)(2,1)} %leaf_inv_h.1, ...), custom_call_target="tpu_custom_call" | custom-call | tf_op jit(solution)/shard_map/pallas_call | solution.py:448
  57.5 0.6 %copy.13 = bf16[4,256,32]{1,2,0:T(8,128)(2,1)} copy(bf16[4,256,32]{1,2,0:T(8,128)(2,1)S(1)} %bitcast.5) | data formatting | bytes 131072
  58.1 1.6 %copy.14 = bf16[7,256,32]{1,2,0:T(8,128)(2,1)} copy(bf16[7,256,32]{1,2,0:T(8,128)(2,1)} %bitcast.7) | data formatting | bytes 229376
Async XLA Ops:
  0.6 0.8 %copy-start = (bf16[4,256,32]{1,2,0:T(8,128)(2,1)S(1)}, bf16[4,256,32]{1,2,0:T(8,128)(2,1)}, u32[]{:S(2)}) copy-start(bf16[4,256,32]{1,2,0:T(8,128)(2,1)} %param.9) | copy-start | bytes 196612
  1.5 0.7 %copy-start.1 = (s32[4]{0:T(128)S(1)}, s32[4]{0:T(128)}, u32[]{:S(2)}) copy-start(s32[4]{0:T(128)} %leaf_widths_h.1) | copy-start | bytes 52
  2.1 0.7 %copy-start.2 = (s32[7]{0:T(128)S(1)}, s32[7]{0:T(128)}, u32[]{:S(2)}) copy-start(s32[7]{0:T(128)} %upper_widths_h.1) | copy-start | bytes 88
